TPU v7x, 256 devices: a whole 4x4x8 slice. The times are simulated.
256 devices in a mesh: node: 32 (over z, y), local: 8 (over x, core).
Axes of the slice: x: 4, y: 4, z: 8, core: 2. Of those that a mesh axis runs over, the one named last changes fastest.
Arguments:
- queries: bfloat16 [262144, 512], P(('node', 'local')), may hold values from -600 to 600
- keys: bfloat16 [262144, 128], P(('node', 'local')), may hold values from -7 to 7
- values: bfloat16 [262144, 128], P(('node', 'local')), may hold values from -6 to 6
- selected: int32 [2048, 3], P(('node', 'local')), may hold values from -1 to 511, as said below
Outputs:
- attended: bfloat16 [262144, 512], P(('node', 'local'))
Inputs may be any that keep to these rules, and one draw needn't show every extreme that they name: `selected`: row t belongs to query tile t. Every entry that is not -1 names a block that lies wholly before the tile's own block, the entries of a row are distinct, and -1 entries stand only after the others. The entries of a row fall in at most two node groups (a node group is 16 consecutive blocks). Over the rows of one device, the entries that fall in one node group are at most 3 and name at most 2 distinct blocks; both bounds are reached in every draw. The entries of the rows of one device fall in at most 8 distinct node groups, or 32 if that is fewer, and some device reaches that number in every draw. Every device outside the first node group has tiles that name blocks of the first node group.
All inputs are finite; a program needn't handle non-finite values.
Results may differ from a plain program's by a relative error of at most 0.0042.
Values may be sent and summed in bfloat16 or wider, within the bound.
A program may use at most 128 MiB of HBM per device.

v0:
```python
import math

import jax
import jax.numpy as jnp
from jax import lax
from jax.sharding import PartitionSpec as P

TILE = 128
BLOCK = 512


def slot_plan(rows, group_blocks, node_count, slot_count):
    entries = rows.reshape(-1)
    entry_count = entries.shape[0]
    usable = entries >= 0
    group_of = jnp.where(usable, entries // group_blocks, -1)
    in_group = jnp.where(usable, entries % group_blocks, -1)
    position = jnp.arange(entry_count)
    earlier = position[None, :] < position[:, None]
    equal_ids = position[:, None] == position[None, :]
    ahead = (group_of[:, None] == group_of[None, :]) & usable[None, :] & earlier
    ranking = jnp.sum(ahead.astype(jnp.int32), axis=1)
    slot_of = jnp.sum(jnp.where(equal_ids & usable[None, :], ranking[None, :], 0), axis=1)
    chosen_mask = group_of[None, None, :] == jnp.arange(node_count)[:, None, None]
    chosen_mask = chosen_mask & (ranking[None, None, :] == jnp.arange(slot_count)[None, :, None])
    chosen_mask = chosen_mask & usable[None, None, :]
    request = jnp.max(jnp.where(chosen_mask, in_group[None, None, :], -1), axis=2)
    return (request, group_of, slot_of, usable)


def body(queries, keys, values, selected):
    head_dim = keys.shape[1]
    head_count = queries.shape[1] // head_dim
    tiles_dev = selected.shape[0]
    tok_rows = keys.shape[0]
    blocks_dev = tok_rows // BLOCK
    node_count = lax.axis_size("node")
    group_blocks = lax.axis_size("local") * blocks_dev
    paired = jnp.concatenate([keys, values], axis=1)
    node_pairs = lax.all_gather(paired, "local", axis=0, tiled=True)
    node_blocks = node_pairs.reshape(group_blocks, BLOCK, 2 * head_dim)
    slot_count = 3
    request, group_of, slot_of, usable = slot_plan(selected, group_blocks, node_count, slot_count)
    incoming = lax.all_to_all(request, "node", split_axis=0, concat_axis=0, tiled=True)
    present = incoming >= 0
    picked = node_blocks[jnp.maximum(incoming, 0)]
    outgoing = jnp.where(present[:, :, None, None], picked, jnp.zeros((), picked.dtype))
    arrived = lax.all_to_all(outgoing, "node", split_axis=0, concat_axis=0, tiled=True)
    flat_arrived = arrived.reshape(node_count * slot_count, BLOCK, 2 * head_dim)
    positions = jnp.where(usable, group_of * slot_count + slot_of, 0)
    chosen = flat_arrived[positions].reshape(tiles_dev, 3 * BLOCK, 2 * head_dim)
    live_keys = jnp.repeat(usable.reshape(tiles_dev, 3), BLOCK, axis=1)
    own_blocks = paired.reshape(blocks_dev, BLOCK, 2 * head_dim)
    query_tiles = queries.reshape(tiles_dev, TILE, head_count, head_dim)
    score_scale = 1.0 / math.sqrt(head_dim)

    def attend(operand):
        tile_q, tile_kv, tile_live, tile_index = operand
        block_number = tile_index * TILE // BLOCK
        own_block = lax.dynamic_index_in_dim(own_blocks, block_number, 0, keepdims=False)
        joined = jnp.concatenate([tile_kv, own_block], axis=0)
        block_start = block_number * BLOCK
        key_pos = block_start + jnp.arange(BLOCK)
        query_pos = tile_index * TILE + jnp.arange(TILE)
        visible = key_pos[None, :] <= query_pos[:, None]
        remote_live = jnp.broadcast_to(tile_live[None, :], (TILE, 3 * BLOCK))
        allowed = jnp.concatenate([remote_live, visible], axis=1)
        scores = jnp.einsum(
            "qhd,kd->hqk", tile_q, joined[:, :head_dim], preferred_element_type=jnp.float32
        )
        scores = scores * score_scale
        scores = jnp.where(allowed[None, :, :], scores, -jnp.inf)
        row_max = jnp.max(scores, axis=2, keepdims=True)
        weights = jnp.exp(scores - row_max)
        row_sum = jnp.sum(weights, axis=2)
        weighted = jnp.einsum(
            "hqk,kd->qhd",
            weights.astype(jnp.bfloat16),
            joined[:, head_dim:],
            preferred_element_type=jnp.float32,
        )
        normed = weighted / jnp.transpose(row_sum)[:, :, None]
        return normed.reshape(TILE, head_count * head_dim).astype(jnp.bfloat16)

    outputs = lax.map(attend, (query_tiles, chosen, live_keys, jnp.arange(tiles_dev)))
    return outputs.reshape(tok_rows, head_count * head_dim)


def solution(mesh):
    return jax.shard_map(
        body,
        mesh=mesh,
        in_specs=(
            P(("node", "local"), None),
            P(("node", "local"), None),
            P(("node", "local"), None),
            P(("node", "local"), None),
        ),
        out_specs=P(("node", "local"), None),
        check_vma=False,
    )
```

profile of v0, /device:TPU:193, one launch (start us, length us, event | category | flops | bytes accessed | tf_op | source)
XLA Modules:
  0.0 756.3 jit_solution(11778456338818622780)
XLA Ops:
  10.7 14.0 %all_to_all.14 = s32[32,1,3]{2,1,0:T(1,128)S(1)} all-to-all(s32[32,1,3]{2,1,0:T(1,128)S(1)} %copy.34), channel_id=1, replica_groups=mesh['node'=32,'local'=8] {'node'}, dimensions={0} | all-to-all | bytes 768 | tf_op jit(solution)/shard_map/all_to_all | solution.py:44
  25.1 20.3 %all-gather.2.cloned.1.call-done = bf16[8192,256]{1,0:T(8,128)(2,1)} async-done(((bf16[1024,256]{1,0:T(8,128)(2,1)}), bf16[8192,256]{1,0:T(8,128)(2,1)}) %all-gather.2.cloned.1.call-update) | async-done | bytes 4194320 | tf_op jit(solution)/shard_map/all_gather | solution.py:40
  45.4 11.9 %gather_fusion = bf16[96,512,256]{2,1,0:T(8,128)(2,1)} fusion(bf16[16,512,256]{2,1,0:T(8,128)(2,1)} %bitcast.61, s32[1024]{0:T(1024)S(1)} %pad_clamp_fusion.1), kind=kCustom, calls=%fused_computation | custom fusion | bytes 50332032 | tf_op jit(solution)/shard_map/gather | solution.py:46
  57.3 20.8 %broadcast_select_fusion = bf16[32,3,512,256]{3,2,1,0:T(8,128)(2,1)} fusion(bf16[32,3,512,256]{3,2,1,0:T(8,128)(2,1)} %bitcast.62, pred[32,3]{1,0:T(8,128)(4,1)S(1)} %copy.36), kind=kLoop, calls=%fused_computation.30 | loop fusion | flops 12582912 | bytes 50331744 | tf_op jit(solution)/shard_map/jit(_where)/select_n | solution.py:47
  78.1 9.3 %all-to-all-start.1 = ((bf16[32,3,512,256]{3,2,1,0:T(8,128)(2,1)}), bf16[32,3,512,256]{3,2,1,0:T(8,128)(2,1)}, u32[]{:S(2)}, u32[]{:S(2)}) async-start(bf16[32,3,512,256]{3,2,1,0:T(8,128)(2,1)} %broadcast_select_fusion), calls=%async_computation.1 | async-start | bytes 50331648 | tf_op jit(solution)/shard_map/all_to_all | solution.py:48
  88.0 598.6 %all-to-all-done.1 = bf16[32,3,512,256]{3,2,1,0:T(8,128)(2,1)} async-done(((bf16[32,3,512,256]{3,2,1,0:T(8,128)(2,1)}), bf16[32,3,512,256]{3,2,1,0:T(8,128)(2,1)}, u32[]{:S(2)}, u32[]{:S(2)}) %all-to-all-start.1) | async-done | bytes 25165856 | tf_op jit(solution)/shard_map/all_to_all | solution.py:48
  686.5 12.8 %gather_fusion.1 = bf16[24,512,256]{2,1,0:T(8,128)(2,1)} fusion(bf16[96,512,256]{2,1,0:T(8,128)(2,1)} %bitcast.14, s32[1024]{0:T(1024)S(1)} %pad_clamp_fusion), kind=kCustom, calls=%fused_computation.1 | custom fusion | bytes 12583008 | tf_op jit(solution)/shard_map/gather | solution.py:51
  699.4 49.0 %while.12 = (s32[]{:T(128)}, bf16[8,128,512]{2,1,0:T(8,128)(2,1)S(1)}, bf16[8,1536,256]{2,1,0:T(8,128)(2,1)}, s32[8]{0:T(128)S(1)}, bf16[2,512,256]{2,1,0:T(8,12...) while((s32[]{:T(128)}, ...), condition=%wide.region_6.7_spmd, body=%wide.region_3.6_spmd.sunk | while | flops 546766464 | bytes 18505612 | solution.py:85
  700.9 1.0 pad_add_fusion.2
  702.0 1.2 dynamic-slice_bitcast_fusion.5
  707.1 1.0 pad_add_fusion.2
  708.1 1.2 dynamic-slice_bitcast_fusion.5
  713.2 1.0 pad_add_fusion.2
  714.2 1.2 dynamic-slice_bitcast_fusion.5
  719.3 1.0 pad_add_fusion.2
  720.4 1.2 dynamic-slice_bitcast_fusion.5
  725.5 1.0 pad_add_fusion.2
  726.5 1.2 dynamic-slice_bitcast_fusion.5
  731.6 1.0 pad_add_fusion.2
  732.6 1.2 dynamic-slice_bitcast_fusion.5
  737.7 1.0 pad_add_fusion.2
  738.8 1.2 dynamic-slice_bitcast_fusion.5
  743.9 1.0 pad_add_fusion.2
  744.9 1.2 dynamic-slice_bitcast_fusion.5
  (144 shorter events, 31.1 us)
Async XLA Ops:
  6.5 38.8 %all-gather.2.cloned.1.call-start = ((), (), s32[]{:S(2)}) async-start(), calls=%async_computation.2 | async-start | bytes 4718592 | tf_op jit(solution)/shard_map/all_gather | solution.py:40
  8.6 0.8 copy-start
  78.1 9.4 %copy-start.2 = (bf16[1024,512]{1,0:T(8,128)(2,1)S(1)}, bf16[1024,512]{1,0:T(8,128)(2,1)}, u32[]{:S(2)}) copy-start(bf16[1024,512]{1,0:T(8,128)(2,1)} %param.6) | copy-start | bytes 3145732
  78.1 9.8 %copy-start.3 = (s32[8,3]{0,1:T(4,128)S(1)}, s32[8,3]{0,1:T(4,128)}, u32[]{:S(2)}) copy-start(s32[8,3]{0,1:T(4,128)} %param.9) | copy-start | bytes 292
  78.1 608.4 %all-to-all-start.1 = ((bf16[32,3,512,256]{3,2,1,0:T(8,128)(2,1)}), bf16[32,3,512,256]{3,2,1,0:T(8,128)(2,1)}, u32[]{:S(2)}, u32[]{:S(2)}) async-start(bf16[32,3,512,256]{3,2,1,0:T(8,128)(2,1)} %broadcast_select_fusion), calls=%async_computation.1 | async-start | bytes 50331648 | tf_op jit(solution)/shard_map/all_to_all | solution.py:48
  686.5 12.9 %copy-start.1 = (bf16[1024,256]{1,0:T(8,128)(2,1)S(1)}, bf16[1024,256]{1,0:T(8,128)(2,1)}, u32[]{:S(2)}) copy-start(bf16[1024,256]{1,0:T(8,128)(2,1)} %copy-done) | copy-start | bytes 1572868
  686.5 12.9 %copy-start.4 = (bf16[8,128,512]{2,1,0:T(8,128)(2,1)S(1)}, bf16[8,128,512]{2,1,0:T(8,128)(2,1)}, u32[]{:S(2)}) copy-start(bf16[8,128,512]{2,1,0:T(8,128)(2,1)} %custom-call.5) | copy-start | bytes 3145732
  748.5 1.0 copy-start.5
Sparse Core Ops, SparseCore 0:
  9.5 35.8 all-gather.1
where the time goes:
time: 767 us; the launch traced here: 756 us
  waiting for transfers between devices  619 us (81%)
  local copies, waits for them, and re-layouts  46.4 us (6%)
  other arithmetic  35.4 us (5%)
  blocking collectives  14 us (2%)
  between operations  13.5 us (2%)
  matrix products  12.6 us (2%)
  starting transfers between devices  9.3 us (1%)
    all_to_all x1, waiting for transfers between devices, body(): lax.all_to_all(outgoing, 'node', split_axis=0, concat_axis=0, tiled=True)  599 us
    select_n x1, other arithmetic, body(): jnp.where(present[:, :, None, None], picked, jnp.zeros((), picked.dtype))  20.8 us
    all_gather x1, waiting for transfers between devices, body(): node_pairs = lax.all_gather(paired, 'local', axis=0, tiled=True)  20.3 us
  transfers between devices with their start and end apart: 2, of which 2 were waited for; matrix products, arithmetic and copies ran while one was open for 0% of the time, Pallas kernels for 0%

commit v1 on v0

v1 whole, which is shorter than its diff:
```python
import functools
import math

import jax
import jax.numpy as jnp
from jax import lax
from jax.experimental import pallas as pl
from jax.experimental.pallas import tpu as pltpu
from jax.sharding import PartitionSpec as P

MESH = pl.DeviceIdType.MESH
BF16 = jnp.bfloat16
F32 = jnp.float32

TILE = 128
BLOCK = 512
HEADS = 4
DIM = 128
NX, NY, NZ = 4, 4, 8
CHIPS = NX * NY
SLOTS = 16
ENTRIES = 24
TILES = 8
UNIT = CHIPS * 2
STORE = NZ * 2 * UNIT
UP_STEPS, DOWN_STEPS = 4, 3
LAST_DOWN = 2
SCALE2 = math.log2(math.e) / math.sqrt(DIM)
DEAD = -1e30

ORDER = [
    (0, 1), (0, 3), (1, 0), (3, 0), (1, 1), (3, 3), (1, 3), (3, 1),
    (0, 2), (2, 0), (2, 2), (1, 2), (3, 2), (2, 1), (2, 3),
]


def device(z, y, x, c):
    return (z * NY + y, x * 2 + c)


def kernel(
    q_ref, k_ref, v_ref, slots_ref, emap_ref, out_ref,
    st0, st1, st2, st3, sb0, sb1, sb2, sb3, rb0, rb1, rb2, rb3,
    req, idxv, idxs, p_ref, m_ref, l_ref, acc_ref,
    rq_send, rq_recv, ix_sem, t_send, t_recv, z_send, z_recv, s_send, s_recv, g_send, g_recv,
):
    store = [st0, st1, st2, st3]
    outgoing = [sb0, sb1, sb2, sb3]
    arrived = [rb0, rb1, rb2, rb3]
    node = lax.axis_index("node")
    local = lax.axis_index("local")
    z, y, x, c = node // NY, node % NY, local // 2, local % 2
    chip = y * NX + x

    def partner(dy, dx):
        return device(z, (y + dy) % NY, (x + dx) % NX, c)

    above = device((z + 1) % NZ, y, x, c)
    below = device((z + NZ - 1) % NZ, y, x, c)
    sibling = device(z, y, x, 1 - c)

    barrier = pltpu.get_barrier_semaphore()
    for dy, dx in ORDER:
        pl.semaphore_signal(barrier, inc=1, device_id=partner(dy, dx), device_id_type=MESH)
    for other in (above, below, sibling):
        pl.semaphore_signal(barrier, inc=1, device_id=other, device_id_type=MESH)
    pl.semaphore_wait(barrier, len(ORDER) + 3)

    for dy, dx in ORDER:
        pltpu.make_async_remote_copy(
            slots_ref, req.at[dy * NX + dx], rq_send, rq_recv,
            device_id=partner(dy, dx), device_id_type=MESH,
        ).start()
    req[0] = slots_ref[...]

    def source(q, piece):
        ref = k_ref if q < 2 else v_ref
        return ref.at[:, piece, q % 2]

    def unit(q, plane, core):
        return store[q].at[pl.ds((plane * 2 + core) * UNIT, UNIT)]

    for q in range(4):
        for dy, dx in ORDER:
            to = ((y + dy) % NY) * NX + (x + dx) % NX
            offset = dy * NX + dx
            pltpu.make_async_remote_copy(
                source(q, to),
                store[q].at[pl.ds((z * 2 + c) * UNIT + offset * 2, 2)],
                t_send.at[q], t_recv.at[q],
                device_id=partner(dy, dx), device_id_type=MESH,
            ).start()
        store[q][pl.ds((z * 2 + c) * UNIT, 2)] = source(q, chip)[...]

    def spread_wait(q):
        rest = store[q].at[pl.ds((z * 2 + c) * UNIT + 2, UNIT - 2)]
        pltpu.make_async_copy(rest, rest, t_recv.at[q]).wait()

    pltpu.make_async_copy(req.at[pl.ds(1, CHIPS - 1)], req.at[pl.ds(1, CHIPS - 1)], rq_recv).wait()
    ids = req[:, 0, :]
    offset_y = (y + NY - (ids // 16) % NY) % NY
    offset_x = (x + NX - (ids // 4) % NX) % NX
    idxv[...] = (ids // 64 * 2 + (ids // 2) % 2) * UNIT + (offset_y * NX + offset_x) * 2 + ids % 2
    fetch = pltpu.make_async_copy(idxv, idxs, ix_sem)
    fetch.start()
    fetch.wait()

    def up_copy(q, t):
        piece = unit(q, z - t, c)
        return pltpu.make_async_remote_copy(
            piece, piece, z_send.at[q, 0, t], z_recv.at[q, 0, t],
            device_id=above, device_id_type=MESH,
        )

    def down_copy(q, t):
        piece = unit(q, (z + t) % NZ, c)
        return pltpu.make_async_remote_copy(
            piece, piece, z_send.at[q, 1, t], z_recv.at[q, 1, t],
            device_id=below, device_id_type=MESH,
        )

    def across_copy(q, plane):
        piece = unit(q, plane, c)
        return pltpu.make_async_remote_copy(
            piece, piece, s_send.at[q, plane], s_recv.at[q, plane],
            device_id=sibling, device_id_type=MESH,
        )

    def sends_up(t):
        return (z - t >= 0) & (z < NZ - 1)

    def sends_down(t):
        return (z + t) % NZ <= LAST_DOWN

    def gets_up(t):
        return z - 1 - t >= 0

    def gets_down(t):
        return (z + 1 + t) % NZ <= LAST_DOWN

    def ring_step(q, t):
        if t == 0:
            spread_wait(q)
        if 1 <= t <= UP_STEPS:
            @pl.when(gets_up(t - 1))
            def _():
                piece = unit(q, z - t, c)
                pltpu.make_async_copy(piece, piece, z_recv.at[q, 0, t - 1]).wait()
        if t < UP_STEPS:
            @pl.when(sends_up(t))
            def _():
                up_copy(q, t).start()
        if 1 <= t <= DOWN_STEPS:
            @pl.when(gets_down(t - 1))
            def _():
                piece = unit(q, (z + t) % NZ, c)
                pltpu.make_async_copy(piece, piece, z_recv.at[q, 1, t - 1]).wait()
        if t < DOWN_STEPS:
            @pl.when(sends_down(t))
            def _():
                down_copy(q, t).start()
        if t == 0:
            across_copy(q, z).start()
        else:
            if t <= UP_STEPS:
                @pl.when(gets_up(t - 1))
                def _():
                    across_copy(q, z - t).start()
            if t <= DOWN_STEPS:
                @pl.when(gets_down(t - 1) & ((z + t) % NZ < z))
                def _():
                    across_copy(q, (z + t) % NZ).start()

    def across_wait(q):
        for plane in range(NZ):
            @pl.when(plane <= z)
            def _():
                piece = unit(q, plane, 1 - c)
                pltpu.make_async_copy(piece, piece, s_recv.at[q, plane]).wait()

    def ring_drain(q):
        for t in range(UP_STEPS):
            @pl.when(sends_up(t))
            def _():
                up_copy(q, t).wait_send()
        for t in range(DOWN_STEPS):
            @pl.when(sends_down(t))
            def _():
                down_copy(q, t).wait_send()
        for plane in range(NZ):
            @pl.when(plane <= z)
            def _():
                across_copy(q, plane).wait_send()

    def gather(q):
        def fill(offset, carry):
            asked = ((NY - offset // NX) % NY) * NX + (NX - offset % NX) % NX
            for s in range(SLOTS):
                outgoing[q][offset, s] = store[q][idxs[asked, s]]
            return carry

        lax.fori_loop(1, CHIPS, fill, 0)
        for s in range(SLOTS):
            arrived[q][0, s] = store[q][idxs[0, s]]
        for dy, dx in ORDER:
            offset = dy * NX + dx
            pltpu.make_async_remote_copy(
                outgoing[q].at[offset], arrived[q].at[offset], g_send.at[q], g_recv.at[q],
                device_id=partner(dy, dx), device_id_type=MESH,
            ).start()

    def gather_wait(q):
        rest = arrived[q].at[pl.ds(1, CHIPS - 1)]
        pltpu.make_async_copy(rest, rest, g_recv.at[q]).wait()

    def stacked(t):
        rows = pl.ds(t * TILE, TILE)
        return jnp.concatenate([q_ref[rows, h * DIM:(h + 1) * DIM] for h in range(HEADS)], axis=0)

    def scores(a, b):
        return lax.dot_general(a, b, (((1,), (1,)), ((), ())), preferred_element_type=F32)

    def own(block, carry):
        for r in range(BLOCK // TILE):
            t = block * (BLOCK // TILE) + r
            width = (r + 1) * TILE
            keys = k_ref[block].reshape(BLOCK, DIM)[:width]
            vals = v_ref[block].reshape(BLOCK, DIM)[:width]
            s = scores(stacked(t), keys)
            row = lax.broadcasted_iota(jnp.int32, s.shape, 0) % TILE + r * TILE
            col = lax.broadcasted_iota(jnp.int32, s.shape, 1)
            s = jnp.where(col <= row, s, -jnp.inf)
            m = jnp.max(s, axis=1, keepdims=True)
            p = jnp.exp2(s * SCALE2 - m * SCALE2)
            m_ref[t] = m
            l_ref[t] = jnp.sum(p, axis=1, keepdims=True)
            acc_ref[t] = jnp.dot(p.astype(BF16), vals, preferred_element_type=F32)
        return carry

    def slot_of(t, e):
        entry = emap_ref[t * 3 + e]
        return jnp.maximum(entry, 0), jnp.where(entry < 0, DEAD, 0.0).astype(F32)

    def remote_keys(t, carry):
        queries = stacked(t)
        m_own = m_ref[t]
        m = m_own
        parts = []
        for e in range(3):
            slot, bias = slot_of(t, e)
            keys = jnp.concatenate(
                [rb0[:, slot].reshape(BLOCK // 2, DIM), rb1[:, slot].reshape(BLOCK // 2, DIM)], axis=0)
            s = scores(queries, keys)
            m = jnp.maximum(m, jnp.max(s, axis=1, keepdims=True) + bias)
            parts.append((s, bias))
        m2 = m * SCALE2
        alpha = jnp.exp2(m_own * SCALE2 - m2)
        total = l_ref[t] * alpha
        for e, (s, bias) in enumerate(parts):
            p = jnp.exp2(s * SCALE2 - (m2 - bias))
            total = total + jnp.sum(p, axis=1, keepdims=True)
            p_ref[t * 3 + e] = p.astype(BF16)
        l_ref[t] = total
        acc_ref[t] = acc_ref[t] * alpha
        return carry

    def remote_values(half, last):
        ref = arrived[2 + half]

        def step(t, carry):
            acc = acc_ref[t]
            for e in range(3):
                slot, _ = slot_of(t, e)
                vals = ref[:, slot].reshape(BLOCK // 2, DIM)
                p = p_ref[t * 3 + e, :, half * (BLOCK // 2):(half + 1) * (BLOCK // 2)]
                acc = acc + jnp.dot(p, vals, preferred_element_type=F32)
            if last:
                normed = (acc / l_ref[t]).astype(BF16)
                for h in range(HEADS):
                    out_ref[pl.ds(t * TILE, TILE), h * DIM:(h + 1) * DIM] = normed[h * TILE:(h + 1) * TILE]
            else:
                acc_ref[t] = acc
            return carry

        lax.fori_loop(0, TILES, step, 0)

    for q in range(4):
        for t in range(UP_STEPS + 1):
            ring_step(q, t)
        if q == 0:
            lax.fori_loop(0, 2, own, 0)
        across_wait(q)
        gather(q)
    gather_wait(0)
    gather_wait(1)
    lax.fori_loop(0, TILES, remote_keys, 0)
    gather_wait(2)
    remote_values(0, False)
    gather_wait(3)
    remote_values(1, True)

    pltpu.make_async_copy(req.at[pl.ds(1, CHIPS - 1)], req.at[pl.ds(1, CHIPS - 1)], rq_send).wait()
    for q in range(4):
        rest = store[q].at[pl.ds(0, UNIT - 2)]
        pltpu.make_async_copy(rest, rest, t_send.at[q]).wait()
        ring_drain(q)
        rest = outgoing[q].at[pl.ds(1, CHIPS - 1)]
        pltpu.make_async_copy(rest, rest, g_send.at[q]).wait()


def plan_slots(selected, first_block):
    entries = selected.reshape(-1)
    count = entries.shape[0]
    position = jnp.arange(count)
    usable = entries >= 0
    same = (entries[:, None] == entries[None, :]) & usable[:, None]
    first = usable & ~jnp.any(same & (position[None, :] < position[:, None]), axis=1)
    rank = jnp.sum((first[None, :] & (position[None, :] < position[:, None])).astype(jnp.int32), axis=1)
    slot = jnp.sum(jnp.where(same & first[None, :], rank[None, :], 0), axis=1)
    slot = jnp.where(usable, slot, -1)
    lanes = jnp.arange(128)
    hit = first[:, None] & (rank[:, None] == lanes[None, :])
    ids = jnp.where(jnp.any(hit, axis=0), jnp.sum(jnp.where(hit, entries[:, None], 0), axis=0), first_block)
    return jnp.broadcast_to(ids[None, :], (8, 128)).astype(jnp.int32), slot.astype(jnp.int32)


def body(queries, keys, values, selected):
    tokens = keys.shape[0]
    plane = lax.axis_index("node") // NY
    slots, emap = plan_slots(selected, plane * (CHIPS * 4))
    view = (tokens // BLOCK, CHIPS, 2, 16, DIM)
    vmem = pl.BlockSpec(memory_space=pltpu.VMEM)
    smem = pl.BlockSpec(memory_space=pltpu.SMEM)
    dma = pltpu.SemaphoreType.DMA
    scratch = (
        [pltpu.VMEM((STORE, 16, DIM), BF16)] * 4
        + [pltpu.VMEM((CHIPS, SLOTS, 16, DIM), BF16)] * 8
        + [
            pltpu.VMEM((CHIPS, 8, 128), jnp.int32),
            pltpu.VMEM((CHIPS, 128), jnp.int32),
            pltpu.SMEM((CHIPS, 128), jnp.int32),
            pltpu.VMEM((TILES * 3, HEADS * TILE, BLOCK), BF16),
            pltpu.VMEM((TILES, HEADS * TILE, 1), F32),
            pltpu.VMEM((TILES, HEADS * TILE, 1), F32),
            pltpu.VMEM((TILES, HEADS * TILE, DIM), F32),
            dma, dma, dma,
            dma((4,)), dma((4,)),
            dma((4, 2, UP_STEPS)), dma((4, 2, UP_STEPS)),
            dma((4, NZ)), dma((4, NZ)),
            dma((4,)), dma((4,)),
        ]
    )
    return pl.pallas_call(
        kernel,
        out_shape=jax.ShapeDtypeStruct(queries.shape, BF16),
        in_specs=[vmem, vmem, vmem, vmem, smem],
        out_specs=vmem,
        scratch_shapes=scratch,
        compiler_params=pltpu.CompilerParams(
            collective_id=0, has_side_effects=True, vmem_limit_bytes=56 << 20),
        cost_estimate=pl.CostEstimate(flops=4 << 30, bytes_accessed=8 << 20, transcendentals=8 << 20),
        name="moba",
    )(queries, keys.reshape(view), values.reshape(view), slots, emap)


def solution(mesh):
    spec = P(("node", "local"), None)
    return jax.shard_map(
        body, mesh=mesh, in_specs=(spec,) * 4, out_specs=spec, check_vma=False)
```

time: 767 us -> 109 us (0.14); the launches traced: 756 us -> 108 us
  waiting for transfers between devices: 619 us -> 0 us
  Pallas kernels: 0 us -> 103 us
  local copies, waits for them, and re-layouts: 46.4 us -> 3.7 us
  other arithmetic: 35.4 us -> 1.3 us
  blocking collectives: 14 us -> 0 us
  between operations: 13.5 us -> 0.03 us
  matrix products: 12.6 us -> 0 us
  starting transfers between devices: 9.3 us -> 0 us
    all_to_all x1 -> x0, waiting for transfers between devices: 599 us -> none  [body(): lax.all_to_all(outgoing, 'node', split_axis=0, concat_axis=0, tiled=True)]
    pallas_call x0 -> x1, Pallas kernels: none -> 103 us  [body(): pl.pallas_call(kernel, out_shape=jax.ShapeDtypeStruct(queries.shape, BF16...]
    gather x2 -> x0, local copies, waits for them, and re-layouts: 24.7 us -> none  [the longest x1 12.8 us: body(): chosen = flat_arrived[positions].reshape(tiles_dev, 3 * BLOCK, 2 * head_dim)]
    all_gather x1 -> x0, waiting for transfers between devices: 20.3 us -> none  [body(): node_pairs = lax.all_gather(paired, 'local', axis=0, tiled=True)]
    select_n x3 -> x2, other arithmetic: 20.9 us -> 0.61 us  [the longest x1 0.6 us: plan_slots(): slot = jnp.where(usable, slot, -1)]
    all_to_all x1 -> x0, blocking collectives: 14 us -> none  [body(): lax.all_to_all(request, 'node', split_axis=0, concat_axis=0, tiled=True)]
    dot_general x16 -> x0, matrix products: 12.6 us -> none  [the longest x8 6.82 us: attend(): jnp.einsum('hqk,kd->qhd', weights.astype(jnp.bfloat16), joined[:, head_di...]
    squeeze x16 -> x0, local copies, waits for them, and re-layouts: 9.72 us -> none  [the longest x8 9.53 us: body(): lax.map(attend, (query_tiles, chosen, live_keys, jnp.arange(tiles_dev)))]
  transfers between devices with their start and end apart: 2 -> 0, of which waited for: 2 -> 0; matrix products, arithmetic and copies ran while one was open for 0% -> 0% of each run, Pallas kernels for 0% -> 0%
where the time goes in v1:
time: 109 us; the launch traced here: 108 us
  Pallas kernels  103 us (94%)
  local copies, waits for them, and re-layouts  3.7 us (3%)
  other arithmetic  1.3 us (1%)
    pallas_call x1, Pallas kernels, body(): pl.pallas_call(kernel, out_shape=jax.ShapeDtypeStruct(queries.shape, BF16...  103 us
    unnamed x4, local copies, waits for them, and re-layouts  3.02 us

profile of v1, /device:TPU:193, one launch (start us, length us, event | category | flops | bytes accessed | tf_op | source)
XLA Modules:
  0.0 108.5 jit_solution(2498620211161702528)
XLA Ops:
  0.0 0.0 copy-start
  0.0 0.7 copy-done
  0.7 0.1 copy.7
  0.8 0.1 reshape.41
  0.9 0.2 fusion.2
  1.1 0.1 convert_reduce_fusion
  1.2 0.2 select_reduce_fusion
  1.4 0.6 broadcast_select_fusion.emap_ref
  2.0 0.1 select_reduce_fusion.1
  2.1 0.1 fusion.4
  2.2 0.6 broadcast_in_dim.52.slots_ref
  2.8 103.5 %moba.1 = bf16[1024,512]{1,0:T(8,128)(2,1)} custom-call(bf16[1024,512]{1,0:T(8,128)(2,1)} %q_ref.1, bf16[2,16,2,16,128]{4,3,2,1,0:T(8,128)(2,1)} %bitcast.2, bf16[2,16,2,16,128]{4,3,2,1,0:T(8,128)(2,1)} %bitcast.3, s32[8,128]{1,0:T(8,128)} %broadcast_in_dim.52.slots_ref, s32[24]{0:T(128)} %broadcast_select_fusion.emap_ref), custom_call_target="tpu_custom_call" | custom-call | flops 4294967296 | bytes 8388608 | tf_op jit(solution)/shard_map/moba/pallas_call | solution.py:353
  106.2 2.3 %copy.9 = bf16[1024,512]{1,0:T(8,128)(2,1)} copy(bf16[1024,512]{1,0:T(8,128)(2,1)} %moba.1) | data formatting | bytes 2097152
  (3 shorter events, 0.0 us)
Async XLA Ops:
  0.0 0.7 copy-start

commit v2 on v1

v2 whole, which is shorter than its diff:
```python
import functools
import math

import jax
import jax.numpy as jnp
from jax import lax
from jax.experimental import pallas as pl
from jax.experimental.pallas import tpu as pltpu
from jax.sharding import PartitionSpec as P

MESH = pl.DeviceIdType.MESH
BF16 = jnp.bfloat16
F32 = jnp.float32

TILE = 128
BLOCK = 512
KHALF = BLOCK // 2
HEADS = 4
DIM = 128
NX, NY, NZ = 4, 4, 8
CHIPS = NX * NY
SLOTS = 16
ENTRIES = 24
TILES = 8
UNIT = CHIPS * 2
STORE = NZ * 2 * UNIT
PIECES = 4
PIECE = UNIT // PIECES
UP_STEPS, DOWN_STEPS = (4, 3) * (PIECES // 2), (3, 4) * (PIECES // 2)
OWN_EVERY = 0.5
AHEAD = 0.3
RING_STEPS = 4
SCALE2 = math.log2(math.e) / math.sqrt(DIM)
DEAD = -1e30

ORDER = [
    (0, 1), (0, 3), (1, 0), (3, 0), (1, 1), (3, 3), (1, 3), (3, 1),
    (0, 2), (2, 0), (2, 2), (1, 2), (3, 2), (2, 1), (2, 3),
]


def device(z, y, x, c):
    return (z * NY + y, x * 2 + c)


def kernel(
    q_hbm, k_hbm, v_hbm, sel_hbm, out_hbm,
    q_ref, k_ref, v_ref, sel_ref, out_ref,
    st0, st1, st2, st3, sb0, sb1, sb2, sb3, rb0, rb1, rb2, rb3,
    emap, wanted, req, idxv, idxs, p_ref, m_ref, l_ref, acc_ref,
    in_sem, out_sem, rq_send, rq_recv, ix_sem, t_send, t_recv, z_send, z_recv, s_recv, g_send, g_recv,
):
    store = [st0, st1, st2, st3]
    outgoing = [sb0, sb1, sb2, sb3]
    arrived = [rb0, rb1, rb2, rb3]
    node = lax.axis_index("node")
    local = lax.axis_index("local")
    z, y, x, c = node // NY, node % NY, local // 2, local % 2
    chip = y * NX + x

    def partner(dy, dx):
        return device(z, (y + dy) % NY, (x + dx) % NX, c)

    above = device((z + 1) % NZ, y, x, c)
    below = device((z + NZ - 1) % NZ, y, x, c)
    sibling = device(z, y, x, 1 - c)

    loads = [
        pltpu.make_async_copy(src, dst, in_sem.at[i])
        for i, (src, dst) in enumerate(
            [(sel_hbm, sel_ref), (k_hbm, k_ref), (v_hbm, v_ref), (q_hbm, q_ref)])
    ]
    barrier = pltpu.get_barrier_semaphore()
    for dy, dx in ORDER:
        pl.semaphore_signal(barrier, inc=1, device_id=partner(dy, dx), device_id_type=MESH)
    for other in (above, below, sibling):
        pl.semaphore_signal(barrier, inc=1, device_id=other, device_id_type=MESH)

    for load in loads:
        load.start()

    loads[0].wait()
    entries = [sel_ref[j % 3, j // 3] for j in range(ENTRIES)]
    lane = lax.broadcasted_iota(jnp.int32, (8, 128), 1)
    ids = jnp.full((8, 128), z * (CHIPS * 4), jnp.int32)
    numbers = []
    count = jnp.int32(0)
    for j, entry in enumerate(entries):
        number, seen = count, entry < 0
        for i in range(j):
            same = entries[i] == entry
            number = jnp.where(same, numbers[i], number)
            seen = seen | same
        number = jnp.where(entry < 0, -1, number)
        count = jnp.where(seen, count, count + 1)
        numbers.append(number)
        emap[j] = number
        ids = jnp.where(lane == number, entry, ids)
    wanted[...] = ids

    loads[1].wait()
    pl.semaphore_wait(barrier, len(ORDER) + 3)

    def source(q, piece):
        ref = k_ref if q < 2 else v_ref
        return ref.at[:, piece, q % 2]

    def spread(q):
        for dy, dx in ORDER:
            to = ((y + dy) % NY) * NX + (x + dx) % NX
            offset = dy * NX + dx
            pltpu.make_async_remote_copy(
                source(q, to),
                store[q].at[pl.ds((c * NZ + z) * UNIT + offset * 2, 2)],
                t_send.at[q], t_recv.at[q, dy],
                device_id=partner(dy, dx), device_id_type=MESH,
            ).start()
        store[q][pl.ds((c * NZ + z) * UNIT, 2)] = source(q, chip)[...]

    def spread_wait(q, h):
        first = 2 if h == 0 else 0
        rest = store[q].at[pl.ds((c * NZ + z) * UNIT + h * PIECE + first, PIECE - first)]
        pltpu.make_async_copy(rest, rest, t_recv.at[q, h]).wait()

    def ask():
        for dy, dx in ORDER:
            pltpu.make_async_remote_copy(
                wanted, req.at[dy * NX + dx], rq_send, rq_recv,
                device_id=partner(dy, dx), device_id_type=MESH,
            ).start()
        req[0] = wanted[...]

    def places():
        rest = req.at[pl.ds(1, CHIPS - 1)]
        pltpu.make_async_copy(rest, rest, rq_recv).wait()
        ids = req[:, 0, :]
        offset_y = (y + NY - (ids // 16) % NY) % NY
        offset_x = (x + NX - (ids // 4) % NX) % NX
        idxv[...] = ((ids // 2) % 2 * NZ + ids // 64) * UNIT + (offset_y * NX + offset_x) * 2 + ids % 2
        pltpu.make_async_copy(idxv, idxs, ix_sem).start()

    def places_wait():
        pltpu.make_async_copy(idxv, idxs, ix_sem).wait()

    def piece(q, plane, core, h):
        return store[q].at[pl.ds((core * NZ + plane) * UNIT + h * PIECE, PIECE)]

    def up_copy(q, t, h):
        ref = piece(q, z - t, c, h)
        return pltpu.make_async_remote_copy(
            ref, ref, z_send.at[q], z_recv.at[q, 0, t, h],
            device_id=above, device_id_type=MESH,
        )

    def down_copy(q, t, h):
        ref = piece(q, (z + t) % NZ, c, h)
        return pltpu.make_async_remote_copy(
            ref, ref, z_send.at[q], z_recv.at[q, 1, t, h],
            device_id=below, device_id_type=MESH,
        )

    def across_copy(q, plane, h):
        ref = piece(q, plane, c, h)
        return pltpu.make_async_remote_copy(
            ref, ref, z_send.at[q], s_recv.at[q],
            device_id=sibling, device_id_type=MESH,
        )

    def sends_up(t):
        return (z - t >= 0) & (z < NZ - 1)

    def sends_down(t, h):
        return (z + t) % NZ < DOWN_STEPS[h]

    def gets_up(t):
        return z - 1 - t >= 0

    def gets_down(t, h):
        return (z + 1 + t) % NZ < DOWN_STEPS[h]

    def ring_step(q, t, h):
        if t == 0:
            spread_wait(q, h)
        if 1 <= t <= UP_STEPS[h]:
            @pl.when(gets_up(t - 1))
            def _():
                ref = piece(q, z - t, c, h)
                pltpu.make_async_copy(ref, ref, z_recv.at[q, 0, t - 1, h]).wait()
        if t < UP_STEPS[h]:
            @pl.when(sends_up(t))
            def _():
                up_copy(q, t, h).start()
        if 1 <= t <= DOWN_STEPS[h]:
            @pl.when(gets_down(t - 1, h))
            def _():
                ref = piece(q, (z + t) % NZ, c, h)
                pltpu.make_async_copy(ref, ref, z_recv.at[q, 1, t - 1, h]).wait()
        if t < DOWN_STEPS[h]:
            @pl.when(sends_down(t, h))
            def _():
                down_copy(q, t, h).start()
        if t == 0:
            across_copy(q, z, h).start()
        else:
            if t <= UP_STEPS[h]:
                @pl.when(gets_up(t - 1))
                def _():
                    across_copy(q, z - t, h).start()
            if t <= DOWN_STEPS[h]:
                @pl.when(gets_down(t - 1, h) & ((z + t) % NZ < z))
                def _():
                    across_copy(q, (z + t) % NZ, h).start()

    def across_wait(q):
        for plane in range(NZ):
            @pl.when(z == plane)
            def _():
                ref = store[q].at[pl.ds((1 - c) * NZ * UNIT, (plane + 1) * UNIT)]
                pltpu.make_async_copy(ref, ref, s_recv.at[q]).wait()

    def ring_drain(q):
        for plane in range(NZ):
            count = 0
            for h in range(PIECES):
                if plane < NZ - 1:
                    count += sum(plane - t >= 0 for t in range(UP_STEPS[h]))
                count += sum((plane + t) % NZ < DOWN_STEPS[h] for t in range(DOWN_STEPS[h]))
            tiles = count * PIECE + (plane + 1) * UNIT

            @pl.when(z == plane)
            def _():
                ref = store[q].at[pl.ds(0, tiles)]
                pltpu.make_async_copy(ref, ref, z_send.at[q]).wait()
        rest = store[q].at[pl.ds(0, UNIT - 2)]
        pltpu.make_async_copy(rest, rest, t_send.at[q]).wait()

    def gather(q, part):
        def fill(offset, carry):
            asked = ((NY - offset // NX) % NY) * NX + (NX - offset % NX) % NX
            for s in range(SLOTS):
                outgoing[q][offset, s] = store[q][idxs[asked, s]]
            return carry

        if part == 0:
            for s in range(SLOTS):
                arrived[q][0, s] = store[q][idxs[0, s]]
        for dy, dx in ORDER[part * 4:part * 4 + 4]:
            offset = dy * NX + dx
            fill(offset, 0)
            pltpu.make_async_remote_copy(
                outgoing[q].at[offset], arrived[q].at[offset], g_send.at[q], g_recv.at[q],
                device_id=partner(dy, dx), device_id_type=MESH,
            ).start()

    def gather_wait(q):
        rest = arrived[q].at[pl.ds(1, CHIPS - 1)]
        pltpu.make_async_copy(rest, rest, g_recv.at[q]).wait()

    def stacked(t):
        rows = pl.ds(t * TILE, TILE)
        return jnp.concatenate([q_ref[rows, h * DIM:(h + 1) * DIM] for h in range(HEADS)], axis=0)

    def scores(a, b):
        return lax.dot_general(a, b, (((1,), (1,)), ((), ())), preferred_element_type=F32)

    def own(t):
        block, r = t // (BLOCK // TILE), t % (BLOCK // TILE)
        width = (r + 1) * TILE
        keys = k_ref[block].reshape(BLOCK, DIM)[:width]
        vals = v_ref[block].reshape(BLOCK, DIM)[:width]
        s = scores(stacked(t), keys)
        row = lax.broadcasted_iota(jnp.int32, s.shape, 0) % TILE + r * TILE
        col = lax.broadcasted_iota(jnp.int32, s.shape, 1)
        s = jnp.where(col <= row, s, -jnp.inf)
        m = jnp.max(s, axis=1, keepdims=True)
        p = jnp.exp2(s * SCALE2 - m * SCALE2)
        m_ref[t] = m
        l_ref[t] = jnp.sum(p, axis=1, keepdims=True)
        acc_ref[t] = jnp.dot(p.astype(BF16), vals, preferred_element_type=F32)

    def slot_of(t, e):
        entry = emap[t * 3 + e]
        return jnp.maximum(entry, 0), jnp.where(entry < 0, DEAD, 0.0).astype(F32)

    def remote_keys(t, carry):
        queries = stacked(t)
        m_own = m_ref[t]
        m = m_own
        parts = []
        for e in range(3):
            slot, bias = slot_of(t, e)
            keys = jnp.concatenate(
                [rb0[:, slot].reshape(KHALF, DIM), rb1[:, slot].reshape(KHALF, DIM)], axis=0)
            s = scores(queries, keys)
            m = jnp.maximum(m, jnp.max(s, axis=1, keepdims=True) + bias)
            parts.append((s, bias))
        m2 = m * SCALE2
        alpha = jnp.exp2(m_own * SCALE2 - m2)
        total = l_ref[t] * alpha
        for e, (s, bias) in enumerate(parts):
            p = jnp.exp2(s * SCALE2 - (m2 - bias))
            total = total + jnp.sum(p, axis=1, keepdims=True)
            p = p.astype(BF16)
            for half in range(2):
                p_ref[half, t, :, e * KHALF:(e + 1) * KHALF] = p[:, half * KHALF:(half + 1) * KHALF]
        l_ref[t] = 1.0 / total
        acc_ref[t] = acc_ref[t] * alpha
        return carry

    def out_copy(rows):
        return pltpu.make_async_copy(out_ref.at[rows], out_hbm.at[rows], out_sem)

    def remote_values(half, last):
        ref = arrived[2 + half]

        def step(t, carry):
            slots = [slot_of(t, e)[0] for e in range(3)]
            vals = jnp.concatenate([ref[:, slot].reshape(KHALF, DIM) for slot in slots], axis=0)
            acc = acc_ref[t] + jnp.dot(p_ref[half, t], vals, preferred_element_type=F32)
            if last:
                normed = (acc * l_ref[t]).astype(out_ref.dtype)
                rows = pl.ds(pl.multiple_of(t * TILE, TILE), TILE)
                for h in range(HEADS):
                    out_ref[rows, h * DIM:(h + 1) * DIM] = normed[h * TILE:(h + 1) * TILE]
                out_copy(rows).start()
            else:
                acc_ref[t] = acc
            return carry

        lax.fori_loop(0, TILES, step, 0)

    spread(0)
    ask()
    spread(1)
    for h in range(PIECES):
        ring_step(0, 0, h)
    loads[2].wait()
    spread(2)
    spread(3)
    loads[3].wait()

    events = []
    for q in range(4):
        begin = 3.5 * q
        for h in range(PIECES):
            if q > 0:
                events.append((begin - AHEAD + h / PIECES, functools.partial(ring_step, q, 0, h)))
            for t in range(1, RING_STEPS + 1):
                events.append((begin + t + h / PIECES, functools.partial(ring_step, q, t, h)))
        events.append((begin + 4.8, functools.partial(across_wait, q)))
        for part in range(4):
            events.append((begin + 4.81 + 0.5 * part * (q < 3), functools.partial(gather, q, part)))
    for t in range(TILES):
        events.append((0.9 + OWN_EVERY * t, functools.partial(own, t)))
    events.append((2.1, places))
    events.append((2.9, places_wait))
    for _, task in sorted(events, key=lambda event: event[0]):
        task()

    gather_wait(0)
    gather_wait(1)
    lax.fori_loop(0, TILES, remote_keys, 0)
    rest = req.at[pl.ds(1, CHIPS - 1)]
    pltpu.make_async_copy(rest, rest, rq_send).wait()
    for q in range(4):
        ring_drain(q)
        if q < 3:
            rest = outgoing[q].at[pl.ds(1, CHIPS - 1)]
            pltpu.make_async_copy(rest, rest, g_send.at[q]).wait()
    gather_wait(2)
    remote_values(0, False)
    gather_wait(3)
    remote_values(1, True)

    out_copy(pl.ds(0, TILES * TILE)).wait()
    rest = outgoing[3].at[pl.ds(1, CHIPS - 1)]
    pltpu.make_async_copy(rest, rest, g_send.at[3]).wait()


def body(queries, keys, values, selected):
    tokens = keys.shape[0]
    view = (tokens // BLOCK, CHIPS, 2, 16, DIM)
    hbm = pl.BlockSpec(memory_space=pl.ANY)
    dma = pltpu.SemaphoreType.DMA
    scratch = (
        [
            pltpu.VMEM(queries.shape, BF16),
            pltpu.VMEM(view, BF16),
            pltpu.VMEM(view, BF16),
            pltpu.SMEM(selected.shape[::-1], jnp.int32),
            pltpu.VMEM(queries.shape, BF16),
        ]
        + [pltpu.VMEM((STORE, 16, DIM), BF16)] * 4
        + [pltpu.VMEM((CHIPS, SLOTS, 16, DIM), BF16)] * 8
        + [
            pltpu.SMEM((ENTRIES,), jnp.int32),
            pltpu.VMEM((8, 128), jnp.int32),
            pltpu.VMEM((CHIPS, 8, 128), jnp.int32),
            pltpu.VMEM((CHIPS, 128), jnp.int32),
            pltpu.SMEM((CHIPS, 128), jnp.int32),
            pltpu.VMEM((2, TILES, HEADS * TILE, 3 * KHALF), BF16),
            pltpu.VMEM((TILES, HEADS * TILE, 1), F32),
            pltpu.VMEM((TILES, HEADS * TILE, 1), F32),
            pltpu.VMEM((TILES, HEADS * TILE, DIM), F32),
            dma((4,)), dma, dma, dma, dma,
            dma((4,)), dma((4, NY)),
            dma((4,)), dma((4, 2, RING_STEPS, PIECES)),
            dma((4,)),
            dma((4,)), dma((4,)),
        ]
    )
    return pl.pallas_call(
        kernel,
        out_shape=jax.ShapeDtypeStruct(queries.shape, BF16),
        in_specs=[hbm] * 4,
        out_specs=hbm,
        scratch_shapes=scratch,
        compiler_params=pltpu.CompilerParams(
            collective_id=0, has_side_effects=True, vmem_limit_bytes=56 << 20),
        cost_estimate=pl.CostEstimate(flops=4 << 30, bytes_accessed=8 << 20, transcendentals=8 << 20),
        name="moba",
    )(queries, keys.reshape(view), values.reshape(view), selected.T)


def solution(mesh):
    spec = P(("node", "local"), None)
    return jax.shard_map(
        body, mesh=mesh, in_specs=(spec,) * 4, out_specs=spec, check_vma=False)
```

time: 109 us -> 82.9 us (0.76)
  Pallas kernels: 103 us -> 80.5 us
  local copies, waits for them, and re-layouts: 3.7 us -> 2.26 us
  other arithmetic: 1.3 us -> 0 us
    pallas_call x1, Pallas kernels: 103 us -> 80.5 us  [body(): pl.pallas_call(kernel, out_shape=jax.ShapeDtypeStruct(queries.shape, BF16...]
    unnamed x4 -> x1, local copies, waits for them, and re-layouts: 3.02 us -> 2.26 us
where the time goes in v2:
time: 82.9 us; the launch traced here: 82.7 us
  Pallas kernels  80.5 us (97%)
  local copies, waits for them, and re-layouts  2.26 us (3%)
    pallas_call x1, Pallas kernels, body(): pl.pallas_call(kernel, out_shape=jax.ShapeDtypeStruct(queries.shape, BF16...  80.5 us
    unnamed x1, local copies, waits for them, and re-layouts  2.26 us

profile of v2, /device:TPU:193, one launch (start us, length us, event | category | flops | bytes accessed | tf_op | source)
XLA Modules:
  0.0 82.7 jit_solution(10335763231005671273)
XLA Ops:
  0.0 80.5 %moba.1 = bf16[1024,512]{1,0:T(8,128)(2,1)} custom-call(bf16[1024,512]{1,0:T(8,128)(2,1)} %q_hbm.1, bf16[2,16,2,16,128]{4,3,2,1,0:T(8,128)(2,1)} %bitcast.3, bf16[2,16,2,16,128]{4,3,2,1,0:T(8,128)(2,1)} %bitcast.4, s32[3,8]{1,0:T(4,128)} %bitcast.5), custom_call_target="tpu_custom_call" | custom-call | flops 4294967296 | bytes 8388608 | tf_op jit(solution)/shard_map/moba/pallas_call | solution.py:412
  80.5 2.3 %copy.6 = bf16[1024,512]{1,0:T(8,128)(2,1)} copy(bf16[1024,512]{1,0:T(8,128)(2,1)} %moba.1) | data formatting | bytes 2097152

commit v3 on v2

--- a/solution.py
+++ b/solution.py
@@ -28,7 +28,6 @@
 PIECE = UNIT // PIECES
 UP_STEPS, DOWN_STEPS = (4, 3) * (PIECES // 2), (3, 4) * (PIECES // 2)
 OWN_EVERY = 0.5
-AHEAD = 0.3
 RING_STEPS = 4
 SCALE2 = math.log2(math.e) / math.sqrt(DIM)
 DEAD = -1e30
@@ -39,16 +38,22 @@
 ]
 
 
+PLACE = {offset: 1 + i for i, offset in enumerate(ORDER)}
+EARLY = 8
+WIDTHS = (KHALF, EARLY * 16, KHALF - EARLY * 16)
+LONG_FIRST = ((0, 2, 1, 3), (1, 3, 0, 2))
+
+
 def device(z, y, x, c):
     return (z * NY + y, x * 2 + c)
 
 
 def kernel(
-    q_hbm, k_hbm, v_hbm, sel_hbm, out_hbm,
-    q_ref, k_ref, v_ref, sel_ref, out_ref,
-    st0, st1, st2, st3, sb0, sb1, sb2, sb3, rb0, rb1, rb2, rb3,
-    emap, wanted, req, idxv, idxs, p_ref, m_ref, l_ref, acc_ref,
-    in_sem, out_sem, rq_send, rq_recv, ix_sem, t_send, t_recv, z_send, z_recv, s_recv, g_send, g_recv,
+    q_hbm, k_hbm, v_hbm, sel_hbm, out_ref,
+    q_ref, k_ref, v_ref, sel_ref,
+    st0, st1, st2, st3, sb0, sb1, sb2, sb3, rb0, rb1, rb2, rb3, rb4,
+    emap, wanted, req, idxv, idxs, p0_ref, p1_ref, p2_ref, m_ref, l_ref, acc_ref,
+    in_sem, rq_send, rq_recv, ix_sem, t_send, t_recv, z_send, z_recv, s_recv, g_send, g_recv,
 ):
     store = [st0, st1, st2, st3]
     outgoing = [sb0, sb1, sb2, sb3]
@@ -178,35 +183,38 @@
     def gets_down(t, h):
         return (z + 1 + t) % NZ < DOWN_STEPS[h]
 
-    def ring_step(q, t, h):
-        if t == 0:
+    spread_seen = set()
+
+    def ring_step(q, t, h, way):
+        if t == 0 and (q, h) not in spread_seen:
+            spread_seen.add((q, h))
             spread_wait(q, h)
-        if 1 <= t <= UP_STEPS[h]:
-            @pl.when(gets_up(t - 1))
-            def _():
-                ref = piece(q, z - t, c, h)
-                pltpu.make_async_copy(ref, ref, z_recv.at[q, 0, t - 1, h]).wait()
-        if t < UP_STEPS[h]:
-            @pl.when(sends_up(t))
-            def _():
-                up_copy(q, t, h).start()
-        if 1 <= t <= DOWN_STEPS[h]:
-            @pl.when(gets_down(t - 1, h))
-            def _():
-                ref = piece(q, (z + t) % NZ, c, h)
-                pltpu.make_async_copy(ref, ref, z_recv.at[q, 1, t - 1, h]).wait()
-        if t < DOWN_STEPS[h]:
-            @pl.when(sends_down(t, h))
-            def _():
-                down_copy(q, t, h).start()
-        if t == 0:
             across_copy(q, z, h).start()
+        if way == 0:
+            if 1 <= t <= UP_STEPS[h]:
+                @pl.when(gets_up(t - 1))
+                def _():
+                    ref = piece(q, z - t, c, h)
+                    pltpu.make_async_copy(ref, ref, z_recv.at[q, 0, t - 1, h]).wait()
+            if t < UP_STEPS[h]:
+                @pl.when(sends_up(t))
+                def _():
+                    up_copy(q, t, h).start()
+            if 1 <= t <= UP_STEPS[h]:
+                @pl.when(gets_up(t - 1))
+                def _():
+                    across_copy(q, z - t, h).start()
         else:
-            if t <= UP_STEPS[h]:
-                @pl.when(gets_up(t - 1))
-                def _():
-                    across_copy(q, z - t, h).start()
-            if t <= DOWN_STEPS[h]:
+            if 1 <= t <= DOWN_STEPS[h]:
+                @pl.when(gets_down(t - 1, h))
+                def _():
+                    ref = piece(q, (z + t) % NZ, c, h)
+                    pltpu.make_async_copy(ref, ref, z_recv.at[q, 1, t - 1, h]).wait()
+            if t < DOWN_STEPS[h]:
+                @pl.when(sends_down(t, h))
+                def _():
+                    down_copy(q, t, h).start()
+            if 1 <= t <= DOWN_STEPS[h]:
                 @pl.when(gets_down(t - 1, h) & ((z + t) % NZ < z))
                 def _():
                     across_copy(q, (z + t) % NZ, h).start()
@@ -234,26 +242,31 @@
         rest = store[q].at[pl.ds(0, UNIT - 2)]
         pltpu.make_async_copy(rest, rest, t_send.at[q]).wait()
 
+    def landing(q, place):
+        if q == 3 and place >= EARLY:
+            return rb4.at[place - EARLY]
+        return arrived[q].at[place]
+
     def gather(q, part):
-        def fill(offset, carry):
-            asked = ((NY - offset // NX) % NY) * NX + (NX - offset % NX) % NX
-            for s in range(SLOTS):
-                outgoing[q][offset, s] = store[q][idxs[asked, s]]
-            return carry
-
         if part == 0:
             for s in range(SLOTS):
                 arrived[q][0, s] = store[q][idxs[0, s]]
         for dy, dx in ORDER[part * 4:part * 4 + 4]:
-            offset = dy * NX + dx
-            fill(offset, 0)
+            place = PLACE[dy, dx]
+            asked = ((NY - dy) % NY) * NX + (NX - dx) % NX
+            for s in range(SLOTS):
+                outgoing[q][place, s] = store[q][idxs[asked, s]]
             pltpu.make_async_remote_copy(
-                outgoing[q].at[offset], arrived[q].at[offset], g_send.at[q], g_recv.at[q],
+                outgoing[q].at[place], landing(q, place),
+                g_send.at[q], g_recv.at[q + 1 if q == 3 and place >= EARLY else q],
                 device_id=partner(dy, dx), device_id_type=MESH,
             ).start()
 
     def gather_wait(q):
-        rest = arrived[q].at[pl.ds(1, CHIPS - 1)]
+        if q == 4:
+            rest = rb4
+        else:
+            rest = arrived[q].at[pl.ds(1, (EARLY if q == 3 else CHIPS) - 1)]
         pltpu.make_async_copy(rest, rest, g_recv.at[q]).wait()
 
     def stacked(t):
@@ -301,39 +314,43 @@
             p = jnp.exp2(s * SCALE2 - (m2 - bias))
             total = total + jnp.sum(p, axis=1, keepdims=True)
             p = p.astype(BF16)
-            for half in range(2):
-                p_ref[half, t, :, e * KHALF:(e + 1) * KHALF] = p[:, half * KHALF:(half + 1) * KHALF]
+            first = 0
+            for p_ref, width in zip((p0_ref, p1_ref, p2_ref), WIDTHS):
+                p_ref[t, :, e * width:(e + 1) * width] = p[:, first:first + width]
+                first += width
         l_ref[t] = 1.0 / total
         acc_ref[t] = acc_ref[t] * alpha
         return carry
 
-    def out_copy(rows):
-        return pltpu.make_async_copy(out_ref.at[rows], out_hbm.at[rows], out_sem)
-
-    def remote_values(half, last):
-        ref = arrived[2 + half]
-
-        def step(t, carry):
+    def remote_values(stage):
+        ref = (rb2, rb3, rb4)[stage]
+        p_ref = (p0_ref, p1_ref, p2_ref)[stage]
+
+        def one(t):
             slots = [slot_of(t, e)[0] for e in range(3)]
-            vals = jnp.concatenate([ref[:, slot].reshape(KHALF, DIM) for slot in slots], axis=0)
-            acc = acc_ref[t] + jnp.dot(p_ref[half, t], vals, preferred_element_type=F32)
-            if last:
-                normed = (acc * l_ref[t]).astype(out_ref.dtype)
+            vals = jnp.concatenate([ref[:, slot].reshape(WIDTHS[stage], DIM) for slot in slots], axis=0)
+            acc = acc_ref[t] + jnp.dot(p_ref[t], vals, preferred_element_type=F32)
+            if stage == 2:
+                normed = (acc * l_ref[t]).astype(BF16)
                 rows = pl.ds(pl.multiple_of(t * TILE, TILE), TILE)
                 for h in range(HEADS):
                     out_ref[rows, h * DIM:(h + 1) * DIM] = normed[h * TILE:(h + 1) * TILE]
-                out_copy(rows).start()
             else:
                 acc_ref[t] = acc
+
+        def step(pair, carry):
+            one(pair * 2)
+            one(pair * 2 + 1)
             return carry
 
-        lax.fori_loop(0, TILES, step, 0)
+        lax.fori_loop(0, TILES // 2, step, 0)
 
     spread(0)
     ask()
     spread(1)
-    for h in range(PIECES):
-        ring_step(0, 0, h)
+    for i in range(PIECES):
+        for way in range(2):
+            ring_step(0, 0, LONG_FIRST[way][i], way)
     loads[2].wait()
     spread(2)
     spread(3)
@@ -342,14 +359,13 @@
     events = []
     for q in range(4):
         begin = 3.5 * q
-        for h in range(PIECES):
-            if q > 0:
-                events.append((begin - AHEAD + h / PIECES, functools.partial(ring_step, q, 0, h)))
-            for t in range(1, RING_STEPS + 1):
-                events.append((begin + t + h / PIECES, functools.partial(ring_step, q, t, h)))
-        events.append((begin + 4.8, functools.partial(across_wait, q)))
+        for i in range(PIECES):
+            for way in range(2):
+                for t in range(0 if q else 1, RING_STEPS + 1):
+                    events.append((begin + t + i / PIECES, functools.partial(ring_step, q, t, LONG_FIRST[way][i], way)))
+        events.append((begin + 4.3, functools.partial(across_wait, q)))
         for part in range(4):
-            events.append((begin + 4.81 + 0.5 * part * (q < 3), functools.partial(gather, q, part)))
+            events.append((begin + 4.31 + 0.5 * part * (q < 3), functools.partial(gather, q, part)))
     for t in range(TILES):
         events.append((0.9 + OWN_EVERY * t, functools.partial(own, t)))
     events.append((2.1, places))
@@ -368,11 +384,12 @@
             rest = outgoing[q].at[pl.ds(1, CHIPS - 1)]
             pltpu.make_async_copy(rest, rest, g_send.at[q]).wait()
     gather_wait(2)
-    remote_values(0, False)
+    remote_values(0)
     gather_wait(3)
-    remote_values(1, True)
-
-    out_copy(pl.ds(0, TILES * TILE)).wait()
+    remote_values(1)
+    gather_wait(4)
+    remote_values(2)
+
     rest = outgoing[3].at[pl.ds(1, CHIPS - 1)]
     pltpu.make_async_copy(rest, rest, g_send.at[3]).wait()
 
@@ -388,32 +405,32 @@
             pltpu.VMEM(view, BF16),
             pltpu.VMEM(view, BF16),
             pltpu.SMEM(selected.shape[::-1], jnp.int32),
-            pltpu.VMEM(queries.shape, BF16),
         ]
         + [pltpu.VMEM((STORE, 16, DIM), BF16)] * 4
-        + [pltpu.VMEM((CHIPS, SLOTS, 16, DIM), BF16)] * 8
+        + [pltpu.VMEM((CHIPS, SLOTS, 16, DIM), BF16)] * 7
+        + [pltpu.VMEM((EARLY, SLOTS, 16, DIM), BF16), pltpu.VMEM((CHIPS - EARLY, SLOTS, 16, DIM), BF16)]
         + [
             pltpu.SMEM((ENTRIES,), jnp.int32),
             pltpu.VMEM((8, 128), jnp.int32),
             pltpu.VMEM((CHIPS, 8, 128), jnp.int32),
             pltpu.VMEM((CHIPS, 128), jnp.int32),
             pltpu.SMEM((CHIPS, 128), jnp.int32),
-            pltpu.VMEM((2, TILES, HEADS * TILE, 3 * KHALF), BF16),
+            *[pltpu.VMEM((TILES, HEADS * TILE, 3 * width), BF16) for width in WIDTHS],
             pltpu.VMEM((TILES, HEADS * TILE, 1), F32),
             pltpu.VMEM((TILES, HEADS * TILE, 1), F32),
             pltpu.VMEM((TILES, HEADS * TILE, DIM), F32),
-            dma((4,)), dma, dma, dma, dma,
+            dma((4,)), dma, dma, dma,
             dma((4,)), dma((4, NY)),
             dma((4,)), dma((4, 2, RING_STEPS, PIECES)),
             dma((4,)),
-            dma((4,)), dma((4,)),
+            dma((4,)), dma((5,)),
         ]
     )
     return pl.pallas_call(
         kernel,
-        out_shape=jax.ShapeDtypeStruct(queries.shape, BF16),
+        out_shape=pltpu.VMEM(queries.shape, BF16),
         in_specs=[hbm] * 4,
-        out_specs=hbm,
+        out_specs=pl.BlockSpec(memory_space=pltpu.VMEM),
         scratch_shapes=scratch,
         compiler_params=pltpu.CompilerParams(
             collective_id=0, has_side_effects=True, vmem_limit_bytes=56 << 20),

time: 82.9 us -> 79.8 us (0.963)
  Pallas kernels: 80.5 us -> 78.3 us
  local copies, waits for them, and re-layouts: 2.26 us -> 0.97 us
    pallas_call x1, Pallas kernels: 80.5 us -> 78.3 us  [body(): pl.pallas_call(kernel, out_shape=pltpu.VMEM(queries.shape, BF16), in_spec...]
    unnamed x1, local copies, waits for them, and re-layouts: 2.26 us -> 0.97 us
where the time goes in v3:
time: 79.8 us; the launch traced here: 79.3 us
  Pallas kernels  78.3 us (98%)
  local copies, waits for them, and re-layouts  0.97 us (1%)
    pallas_call x1, Pallas kernels, body(): pl.pallas_call(kernel, out_shape=pltpu.VMEM(queries.shape, BF16), in_spec...  78.3 us

profile of v3, /device:TPU:193, one launch (start us, length us, event | category | flops | bytes accessed | tf_op | source)
XLA Modules:
  0.0 79.3 jit_solution(3523361761724835080)
XLA Ops:
  0.0 78.3 %moba.1 = bf16[1024,512]{1,0:T(8,128)(2,1)S(1)} custom-call(bf16[1024,512]{1,0:T(8,128)(2,1)} %q_hbm.1, bf16[2,16,2,16,128]{4,3,2,1,0:T(8,128)(2,1)} %bitcast.3, bf16[2,16,2,16,128]{4,3,2,1,0:T(8,128)(2,1)} %bitcast.4, s32[3,8]{1,0:T(4,128)} %bitcast.5), custom_call_target="tpu_custom_call" | custom-call | flops 4294967296 | bytes 8388608 | tf_op jit(solution)/shard_map/moba/pallas_call | solution.py:429
  78.3 1.0 %copy.6 = bf16[1024,512]{1,0:T(8,128)(2,1)} copy(bf16[1024,512]{1,0:T(8,128)(2,1)S(1)} %moba.1) | data formatting | bytes 2097152

commit v4 on v3

--- a/solution.py
+++ b/solution.py
@@ -28,6 +28,7 @@
 PIECE = UNIT // PIECES
 UP_STEPS, DOWN_STEPS = (4, 3) * (PIECES // 2), (3, 4) * (PIECES // 2)
 OWN_EVERY = 0.5
+KEYS_EARLY, KEYS_AT, KEYS_EVERY = 3, 13.4, 0.45
 RING_STEPS = 4
 SCALE2 = math.log2(math.e) / math.sqrt(DIM)
 DEAD = -1e30
@@ -368,14 +369,16 @@
             events.append((begin + 4.31 + 0.5 * part * (q < 3), functools.partial(gather, q, part)))
     for t in range(TILES):
         events.append((0.9 + OWN_EVERY * t, functools.partial(own, t)))
+    events.append((KEYS_AT - 0.02, functools.partial(gather_wait, 0)))
+    events.append((KEYS_AT - 0.01, functools.partial(gather_wait, 1)))
+    for t in range(KEYS_EARLY):
+        events.append((KEYS_AT + KEYS_EVERY * t, functools.partial(remote_keys, t, 0)))
     events.append((2.1, places))
     events.append((2.9, places_wait))
     for _, task in sorted(events, key=lambda event: event[0]):
         task()
 
-    gather_wait(0)
-    gather_wait(1)
-    lax.fori_loop(0, TILES, remote_keys, 0)
+    lax.fori_loop(KEYS_EARLY, TILES, remote_keys, 0)
     rest = req.at[pl.ds(1, CHIPS - 1)]
     pltpu.make_async_copy(rest, rest, rq_send).wait()
     for q in range(4):

time: 79.8 us -> 78.7 us (0.986)
  Pallas kernels: 78.3 us -> 77.5 us
    pallas_call x1, Pallas kernels: 78.3 us -> 77.5 us  [body(): pl.pallas_call(kernel, out_shape=pltpu.VMEM(queries.shape, BF16), in_spec...]
where the time goes in v4:
time: 78.7 us; the launch traced here: 78.5 us
  Pallas kernels  77.5 us (98%)
  local copies, waits for them, and re-layouts  0.97 us (1%)
    pallas_call x1, Pallas kernels, body(): pl.pallas_call(kernel, out_shape=pltpu.VMEM(queries.shape, BF16), in_spec...  77.5 us

profile of v4, /device:TPU:193, one launch (start us, length us, event | category | flops | bytes accessed | tf_op | source)
XLA Modules:
  0.0 78.5 jit_solution(15183819816434477545)
XLA Ops:
  0.0 77.5 %moba.1 = bf16[1024,512]{1,0:T(8,128)(2,1)S(1)} custom-call(bf16[1024,512]{1,0:T(8,128)(2,1)} %q_hbm.1, bf16[2,16,2,16,128]{4,3,2,1,0:T(8,128)(2,1)} %bitcast.3, bf16[2,16,2,16,128]{4,3,2,1,0:T(8,128)(2,1)} %bitcast.4, s32[3,8]{1,0:T(4,128)} %bitcast.5), custom_call_target="tpu_custom_call" | custom-call | flops 4294967296 | bytes 8388608 | tf_op jit(solution)/shard_map/moba/pallas_call | solution.py:432
  77.5 1.0 %copy.6 = bf16[1024,512]{1,0:T(8,128)(2,1)} copy(bf16[1024,512]{1,0:T(8,128)(2,1)S(1)} %moba.1) | data formatting | bytes 2097152

commit v5 on v4

--- a/solution.py
+++ b/solution.py
@@ -28,7 +28,7 @@
 PIECE = UNIT // PIECES
 UP_STEPS, DOWN_STEPS = (4, 3) * (PIECES // 2), (3, 4) * (PIECES // 2)
 OWN_EVERY = 0.5
-KEYS_EARLY, KEYS_AT, KEYS_EVERY = 3, 13.4, 0.45
+KEYS_EARLY, KEYS_AT, KEYS_EVERY = 2, 13.4, 0.6
 RING_STEPS = 4
 SCALE2 = math.log2(math.e) / math.sqrt(DIM)
 DEAD = -1e30
@@ -378,7 +378,12 @@
     for _, task in sorted(events, key=lambda event: event[0]):
         task()
 
-    lax.fori_loop(KEYS_EARLY, TILES, remote_keys, 0)
+    def key_pair(i, carry):
+        remote_keys(KEYS_EARLY + 2 * i, 0)
+        remote_keys(KEYS_EARLY + 2 * i + 1, 0)
+        return carry
+
+    lax.fori_loop(0, (TILES - KEYS_EARLY) // 2, key_pair, 0)
     rest = req.at[pl.ds(1, CHIPS - 1)]
     pltpu.make_async_copy(rest, rest, rq_send).wait()
     for q in range(4):

time: 78.7 us -> 78.9 us (level)
  no operation moved by 1% of the time
where the time goes in v5:
time: 78.9 us; the launch traced here: 78.5 us
  Pallas kernels  77.5 us (98%)
  local copies, waits for them, and re-layouts  0.97 us (1%)
    pallas_call x1, Pallas kernels, body(): pl.pallas_call(kernel, out_shape=pltpu.VMEM(queries.shape, BF16), in_spec...  77.5 us

profile of v5, /device:TPU:193, one launch (start us, length us, event | category | flops | bytes accessed | tf_op | source)
XLA Modules:
  0.0 78.5 jit_solution(7827293846781460735)
XLA Ops:
  0.0 77.5 %moba.1 = bf16[1024,512]{1,0:T(8,128)(2,1)S(1)} custom-call(bf16[1024,512]{1,0:T(8,128)(2,1)} %q_hbm.1, bf16[2,16,2,16,128]{4,3,2,1,0:T(8,128)(2,1)} %bitcast.3, bf16[2,16,2,16,128]{4,3,2,1,0:T(8,128)(2,1)} %bitcast.4, s32[3,8]{1,0:T(4,128)} %bitcast.5), custom_call_target="tpu_custom_call" | custom-call | flops 4294967296 | bytes 8388608 | tf_op jit(solution)/shard_map/moba/pallas_call | solution.py:437
  77.5 1.0 %copy.6 = bf16[1024,512]{1,0:T(8,128)(2,1)} copy(bf16[1024,512]{1,0:T(8,128)(2,1)S(1)} %moba.1) | data formatting | bytes 2097152
